TPU v7x, 32 devices: a whole 2x2x4 slice. The times are simulated.
32 devices in a mesh: groups: 2 (over x), seq: 8 (over z, y), head: 2 (over core).
Axes of the slice: x: 2, y: 2, z: 4, core: 2. Of those that a mesh axis runs over, the one named last changes fastest.
Arguments:
- byte_ids: int32 [8192], P(('groups', 'seq')), parts along dimension 0, may hold values from 0 to 255
- embed_table: bfloat16 [256, 1024], P(None, 'head'), may hold values from -6 to 6
- gains: float32 [2, 1024], replicated, may hold values from 0.1 to 1.9
- conv_weight: bfloat16 [2, 3, 1024, 1024], P(None, None, None, 'head'), may hold values from -0.109375 to 0.109375
- conv_bias: float32 [2, 1024], P(None, 'head'), may hold values from -3 to 3
- qkv_weight: bfloat16 [3, 1024, 2048], P(None, None, 'head'), may hold values from -5 to 5
Outputs:
- context: bfloat16 [1024, 2048], P(('groups', 'seq'), 'head'), parts along dimension 0
There are 2 independent parts, one for each index of `groups`. A program takes and returns all parts, laid end to end along the dimension named above; an argument that names none is the same for every part. Nothing has to cross between parts.
All inputs are finite; a program needn't handle non-finite values.
Results may differ from a plain program's by a relative error of at most 0.0173.
The roundings to bfloat16 on the way count: a program that leaves them out, or rounds other values in their place, can miss the bound.
Values may be sent and summed in bfloat16 or wider, within the bound.
A program may use at most 128 MiB of HBM per device.

v0:
```python
import jax
import jax.numpy as jnp
from jax import lax
from jax.sharding import PartitionSpec as P

D = 1024
HEAD_SIZE = 64
LAYERS = 2
DILATION_FIRST = 1024
DILATION_SECOND = 2048
POOL = 8
epsilon = 1e-05


def activate(stream, gain_row, squares):
    rescale = lax.rsqrt(squares / D + epsilon)
    return jax.nn.gelu(stream * rescale[:, None] * gain_row[None, :], approximate=False).astype(
        jnp.bfloat16
    )


def slide(rows, amount):
    padding = jnp.zeros((abs(amount), rows.shape[1]), rows.dtype)
    if amount > 0:
        return jnp.concatenate([padding, rows[:-amount]], axis=0)
    return jnp.concatenate([rows[-amount:], padding], axis=0)


def attend(running, key_rows, value_rows, queries, query_pos, key_pos):
    row_max, totals, weighted = running
    heads_here = queries.shape[1]
    key_count = key_rows.shape[0]
    key_heads = key_rows.reshape(key_count, heads_here, HEAD_SIZE)
    value_heads = value_rows.reshape(key_count, heads_here, HEAD_SIZE)
    scores = jnp.einsum(
        "qhd,khd->hqk", queries, key_heads, preferred_element_type=jnp.float32
    ) * HEAD_SIZE ** (-0.5)
    visible = key_pos[None, None, :] <= query_pos[None, :, None]
    masked = jnp.where(visible, scores, -1e30)
    new_max = jnp.maximum(row_max, jnp.max(masked, axis=2))
    powers = jnp.where(visible, jnp.exp(masked - new_max[:, :, None]), 0.0)
    totals = jnp.sum(powers, axis=2)
    weighted = jnp.einsum("hqk,khd->hqd", powers, value_heads.astype(jnp.float32))
    return (new_max, totals, weighted)


def local(byte_ids, embed_table, gains, conv_weight, conv_bias, qkv_weight):
    row_count = byte_ids.shape[0]
    width_half = embed_table.shape[1]
    seq_count = lax.axis_size("seq")
    seq_place = lax.axis_index("seq")
    stride_cells = DILATION_FIRST // seq_count
    stride_pooled = stride_cells // POOL
    pooled_rows = row_count // POOL
    all_ids = lax.all_gather(byte_ids, "seq", axis=0, tiled=True)
    all_ids = all_ids.reshape(-1, seq_count, stride_cells)
    local_ids = lax.dynamic_slice_in_dim(all_ids, seq_place, 1, 1).reshape(row_count)
    vocab_ids = jnp.arange(embed_table.shape[0], dtype=jnp.int32)
    one_hot = (local_ids[:, None] == vocab_ids[None, :]).astype(jnp.bfloat16)
    stream = jnp.dot(one_hot, embed_table, preferred_element_type=jnp.float32)
    dilation_list = (DILATION_FIRST, DILATION_SECOND)
    for layer_index in range(LAYERS):
        local_step = dilation_list[layer_index] // DILATION_FIRST * stride_cells
        whole_rows = lax.all_gather(stream, "head", axis=1, tiled=True)
        active = activate(whole_rows, gains[layer_index], jnp.sum(whole_rows * whole_rows, axis=1))
        behind = slide(active, local_step)
        in_front = slide(active, -local_step)
        mixed = jnp.dot(behind, conv_weight[layer_index, 0], preferred_element_type=jnp.float32)
        mixed = mixed + jnp.dot(
            active, conv_weight[layer_index, 1], preferred_element_type=jnp.float32
        )
        mixed = mixed + jnp.dot(
            in_front, conv_weight[layer_index, 2], preferred_element_type=jnp.float32
        )
        stream = stream + mixed + conv_bias[layer_index][None, :]
    pooled = jnp.mean(stream.reshape(pooled_rows, POOL, width_half), axis=1).astype(jnp.bfloat16)
    pooled_full = lax.all_gather(pooled, "head", axis=1, tiled=True)
    heads_here = qkv_weight.shape[2] // HEAD_SIZE
    queries = jnp.dot(pooled_full, qkv_weight[0], preferred_element_type=jnp.float32).astype(
        jnp.bfloat16
    )
    queries = queries.reshape(pooled_rows, heads_here, HEAD_SIZE)
    period = DILATION_FIRST // POOL

    def key_places(offset, count):
        rows_here = offset + jnp.arange(count, dtype=jnp.int32)
        source = rows_here // pooled_rows
        inner = rows_here % pooled_rows
        return inner // stride_pooled * period + source * stride_pooled + inner % stride_pooled

    query_pos = key_places(seq_place * pooled_rows, pooled_rows)
    start_state = (
        jnp.full((heads_here, pooled_rows), -1e30, jnp.float32),
        jnp.zeros((heads_here, pooled_rows), jnp.float32),
        jnp.zeros((heads_here, pooled_rows, HEAD_SIZE), jnp.float32),
    )
    key_rows = jnp.dot(pooled_full, qkv_weight[1], preferred_element_type=jnp.float32).astype(
        jnp.bfloat16
    )
    value_rows = jnp.dot(pooled_full, qkv_weight[2], preferred_element_type=jnp.float32).astype(
        jnp.bfloat16
    )
    pieces = (
        lax.all_gather(key_rows, "seq", axis=0, tiled=True),
        lax.all_gather(value_rows, "seq", axis=0, tiled=True),
    )
    row_max, totals, weighted = attend(
        start_state,
        pieces[0],
        pieces[1],
        queries,
        query_pos,
        key_places(jnp.int32(0), pieces[0].shape[0]),
    )
    out_width = heads_here * HEAD_SIZE
    context = (weighted / totals[:, :, None]).transpose(1, 0, 2).reshape(pooled_rows, out_width)
    context = context.astype(jnp.bfloat16)
    block_count = pooled_rows // stride_pooled
    fan_count = seq_count // block_count
    target = seq_place * stride_pooled // pooled_rows
    picked_dilation = jnp.arange(fan_count, dtype=jnp.int32) == target
    sectioned = jnp.where(
        picked_dilation[None, :, None, None],
        context.reshape(block_count, 1, stride_pooled, out_width),
        jnp.zeros((), jnp.bfloat16),
    )
    sectioned = sectioned.reshape(seq_count * stride_pooled, out_width)
    arrived = lax.all_to_all(sectioned, "seq", split_axis=0, concat_axis=0, tiled=True)
    arrived = arrived.reshape(seq_count, stride_pooled, out_width)
    context = lax.dynamic_slice_in_dim(arrived, seq_place % fan_count * block_count, block_count, 0)
    context = context.reshape(pooled_rows, out_width)
    return context


def solution(mesh):
    placed = (
        P(("groups", "seq")),
        P(None, "head"),
        P(),
        P(None, None, None, "head"),
        P(None, "head"),
        P(None, None, "head"),
    )
    return jax.shard_map(
        local, mesh=mesh, in_specs=placed, out_specs=P(("groups", "seq"), "head"), check_vma=False
    )
```

profile of v0, /device:TPU:0, one launch (start us, length us, event | category | flops | bytes accessed | tf_op | source)
XLA Modules:
  0.0 191.9 jit_solution(12096868458623567444)
XLA Ops:
  6.6 28.1 %all-gather = s32[8,1,512]{2,1,0:T(1,128)S(1)} all-gather(s32[1,1,512]{2,1,0:T(1,128)} %bitcast.72), channel_id=1, replica_groups=mesh['groups'=2,'seq'=8,'head'=2] {'seq'}, dimensions={0}, use_global_device_ids=true | all-gather | bytes 18432 | tf_op jit(solution)/shard_map/all_gather | solution.py:55
  34.6 1.3 fusion.73
  36.1 9.9 %all-gather.6.cloned.1.call-done = f32[512,1024]{1,0:T(8,128)} async-done(((f32[512,512]{1,0:T(8,128)}), f32[512,1024]{1,0:T(8,128)}) %all-gather.6.cloned.1.call-update) | async-done | bytes 2097168 | tf_op jit(solution)/shard_map/all_gather | solution.py:64
  46.0 2.0 %multiply_reduce_fusion.1 = f32[512]{0:T(512)S(1)} fusion(f32[512,1024]{1,0:T(8,128)} %all-gather.6.cloned.1.call-done), kind=kLoop, calls=%fused_computation.48 | loop fusion | flops 1048064 | bytes 2099200 | tf_op jit(solution)/shard_map/reduce_sum | solution.py:65
  48.2 5.1 %fusion.2 = bf16[512,1024]{1,0:T(8,128)(2,1)S(1)} fusion(f32[512,1024]{1,0:T(8,128)S(1)} %copy-done.2, f32[1024]{0:T(1024)S(1)} %bitcast.68, f32[512]{0:T(512)S(1)} %add_rsqrt_fusion.1), kind=kLoop, calls=%fused_computation.4 | loop fusion | flops 35127296 | bytes 3151872 | tf_op jit(solution)/shard_map/convert_element_type | solution.py:17
  55.4 1.7 fusion.34
  57.2 11.9 %all-gather.8.cloned.1.call-done = f32[512,1024]{1,0:T(8,128)} async-done(((f32[512,512]{1,0:T(8,128)}), f32[512,1024]{1,0:T(8,128)}) %all-gather.8.cloned.1.call-update) | async-done | bytes 2097168 | tf_op jit(solution)/shard_map/all_gather | solution.py:64
  69.1 2.0 %multiply_reduce_fusion = f32[512]{0:T(512)S(1)} fusion(f32[512,1024]{1,0:T(8,128)} %all-gather.8.cloned.1.call-done), kind=kLoop, calls=%fused_computation.33 | loop fusion | flops 1048064 | bytes 2099200 | tf_op jit(solution)/shard_map/reduce_sum | solution.py:65
  71.3 5.1 %fusion.5 = bf16[512,1024]{1,0:T(8,128)(2,1)S(1)} fusion(f32[512,1024]{1,0:T(8,128)S(1)} %copy-done.3, f32[1024]{0:T(1024)S(1)} %bitcast.67, f32[512]{0:T(512)S(1)} %add_rsqrt_fusion), kind=kLoop, calls=%fused_computation.7 | loop fusion | flops 35127296 | bytes 3151872 | tf_op jit(solution)/shard_map/convert_element_type | solution.py:17
  76.4 1.9 %fusion.52 = f32[512,512]{1,0:T(8,128)S(1)} fusion(bf16[2,3,1024,512]{3,2,1,0:T(8,128)(2,1)} %param.9, bf16[256,1024]{1,0:T(8,128)(2,1)S(1)} %get-tuple-element.6), kind=kOutput, calls=%fused_computation.74 | convolution fusion | flops 536870912 | bytes 2621440 | tf_op jit(solution)/shard_map/dot_general | solution.py:68
  78.4 2.0 %convolution_add_fusion.1 = f32[512,512]{1,0:T(8,128)S(1)} fusion(f32[512,512]{1,0:T(8,128)S(1)} %fusion.52, bf16[512,1024]{1,0:T(8,128)(2,1)S(1)} %fusion.5, bf16[2,3,1024,512]{3,2,1,0:T(8,128)(2,1)} %param.9), kind=kOutput, calls=%fused_computation.58 | convolution fusion | flops 537133056 | bytes 4194304 | tf_op jit(solution)/shard_map/dot_general | solution.py:69
  80.4 2.2 %fusion.37 = f32[64,512]{1,0:T(8,128)S(1)} fusion(f32[512,512]{1,0:T(8,128)S(1)} %copy-done.4, f32[512,512]{1,0:T(8,128)S(1)} %convolution_add_fusion.1, bf16[2,3,1024,512]{3,2,1,0:T(8,128)(2,1)} %param.9, bf16[256,1024]{1,0:T(8,128)(2,1)S(1)} %get-tuple-element.5, f32[512]{0:T(512)S(1)} %bitcast.73), kind=kOutput, calls=%fused_computation.65 | convolution fusion | flops 537886720 | bytes 3803136 | tf_op jit(solution)/shard_map/dot_general | solution.py:72
  82.6 1.9 all_gather.21
  84.5 2.7 %fusion.42 = bf16[64,1024]{1,0:T(8,128)(2,1)} fusion(bf16[64,1024]{1,0:T(8,128)(2,1)S(1)} %all_gather.21, bf16[3,1024,1024]{2,1,0:T(8,128)(2,1)} %param.11), kind=kOutput, calls=%fused_computation.68 | convolution fusion | flops 134283264 | bytes 2359296 | tf_op jit(solution)/shard_map/dot_general | solution.py:97
  87.5 2.7 %fusion.45 = bf16[64,1024]{1,0:T(8,128)(2,1)} fusion(bf16[64,1024]{1,0:T(8,128)(2,1)S(1)} %all_gather.21, bf16[3,1024,1024]{2,1,0:T(8,128)(2,1)} %param.11), kind=kOutput, calls=%fused_computation.69 | convolution fusion | flops 134283264 | bytes 2359296 | tf_op jit(solution)/shard_map/dot_general | solution.py:100
  90.5 2.1 %fusion.39 = bf16[64,1024]{1,0:T(8,128)(2,1)S(1)} fusion(bf16[64,1024]{1,0:T(8,128)(2,1)S(1)} %all_gather.21, bf16[3,1024,1024]{2,1,0:T(8,128)(2,1)} %param.11), kind=kOutput, calls=%fused_computation.67 | convolution fusion | flops 134283264 | bytes 2359296 | tf_op jit(solution)/shard_map/dot_general | solution.py:79
  92.6 0.9 reshape.205
  93.5 35.3 %all-gather.10.cloned.1.call-done = bf16[512,1024]{1,0:T(8,128)(2,1)} async-done(((bf16[64,1024]{1,0:T(8,128)(2,1)}), bf16[512,1024]{1,0:T(8,128)(2,1)}) %all-gather.10.cloned.1.call-update) | async-done | bytes 1048592 | tf_op jit(solution)/shard_map/all_gather | solution.py:104
  128.7 1.5 copy.14
  130.2 1.5 fusion.29
  132.4 37.2 %all-gather.12.cloned.1.call-done = bf16[512,1024]{1,0:T(8,128)(2,1)} async-done(((bf16[64,1024]{1,0:T(8,128)(2,1)}), bf16[512,1024]{1,0:T(8,128)(2,1)}) %all-gather.12.cloned.1.call-update) | async-done | bytes 1048592 | tf_op jit(solution)/shard_map/all_gather | solution.py:105
  169.7 1.5 copy.16
  173.0 3.4 %all-to-all-start = ((bf16[8,16,1024]{2,1,0:T(8,128)(2,1)}), bf16[8,16,1024]{2,1,0:T(8,128)(2,1)S(1)}, u32[]{:S(2)}, u32[]{:S(2)}) async-start(bf16[8,16,1024]{2,1,0:T(8,128)(2,1)} %bitcast_select_fusion), calls=%async_computation | async-start | bytes 524288 | tf_op jit(solution)/shard_map/all_to_all | solution.py:128
  176.5 8.3 %all-to-all-done = bf16[8,16,1024]{2,1,0:T(8,128)(2,1)S(1)} async-done(((bf16[8,16,1024]{2,1,0:T(8,128)(2,1)}), bf16[8,16,1024]{2,1,0:T(8,128)(2,1)S(1)}, u32[]{:S(2)}, u32[]{:S(2)}) %all-to-all-start) | async-done | bytes 262176 | tf_op jit(solution)/shard_map/all_to_all | solution.py:128
  (47 shorter events, 6.6 us)
Async XLA Ops:
  6.5 28.1 %copy-start = (bf16[256,512]{1,0:T(8,128)(2,1)S(1)}, bf16[256,512]{1,0:T(8,128)(2,1)}, u32[]{:S(2)}) copy-start(bf16[256,512]{1,0:T(8,128)(2,1)} %param.7) | copy-start | bytes 786436
  6.5 29.5 %copy-start.7 = (f32[2,512]{1,0:T(2,128)S(1)}, f32[2,512]{1,0:T(2,128)}, u32[]{:S(2)}) copy-start(f32[2,512]{1,0:T(2,128)} %param.10) | copy-start | bytes 12292
  6.5 29.5 %copy-start.6 = (f32[2,1024]{1,0:T(2,128)S(1)}, f32[2,1024]{1,0:T(2,128)}, u32[]{:S(2)}) copy-start(f32[2,1024]{1,0:T(2,128)} %param.8) | copy-start | bytes 24580
  6.5 39.5 %all-gather.6.cloned.1.call-start = ((), (), s32[]{:S(2)}) async-start(), calls=%async_computation.1 | async-start | bytes 3145728 | tf_op jit(solution)/shard_map/all_gather | solution.py:64
  36.0 33.1 %all-gather.8.cloned.1.call-start = ((), (), s32[]{:S(2)}) async-start(), calls=%async_computation.2 | async-start | bytes 3145728 | tf_op jit(solution)/shard_map/all_gather | solution.py:64
  46.0 2.2 %copy-start.2 = (f32[512,1024]{1,0:T(8,128)S(1)}, f32[512,1024]{1,0:T(8,128)}, u32[]{:S(2)}) copy-start(f32[512,1024]{1,0:T(8,128)} %all-gather.6.cloned.1.call-done) | copy-start | bytes 6291460
  48.2 5.3 %copy-start.5 = (bf16[2,3,1024,512]{3,2,1,0:T(8,128)(2,1)S(1)}, bf16[2,3,1024,512]{3,2,1,0:T(8,128)(2,1)}, u32[]{:S(2)}) copy-start(bf16[2,3,1024,512]{3,2,1,0:T(8,128)(2,1)} %param.9) | copy-start | bytes 18874372
  54.2 1.2 copy-start.1
  57.1 71.6 %all-gather.10.cloned.1.call-start = ((), (), s32[]{:S(2)}) async-start(), calls=%async_computation.3 | async-start | bytes 1179648 | tf_op jit(solution)/shard_map/all_gather | solution.py:104
  69.1 2.2 %copy-start.3 = (f32[512,1024]{1,0:T(8,128)S(1)}, f32[512,1024]{1,0:T(8,128)}, u32[]{:S(2)}) copy-start(f32[512,1024]{1,0:T(8,128)} %all-gather.8.cloned.1.call-done) | copy-start | bytes 6291460
  78.4 2.0 %copy-start.4 = (f32[512,512]{1,0:T(8,128)S(1)}, f32[512,512]{1,0:T(8,128)}, u32[]{:S(2)}) copy-start(f32[512,512]{1,0:T(8,128)} %fusion.34) | copy-start | bytes 3145732
  87.3 82.4 %all-gather.12.cloned.1.call-start = ((), (), s32[]{:S(2)}) async-start(), calls=%async_computation.4 | async-start | bytes 1179648 | tf_op jit(solution)/shard_map/all_gather | solution.py:105
  173.0 11.7 %all-to-all-start = ((bf16[8,16,1024]{2,1,0:T(8,128)(2,1)}), bf16[8,16,1024]{2,1,0:T(8,128)(2,1)S(1)}, u32[]{:S(2)}, u32[]{:S(2)}) async-start(bf16[8,16,1024]{2,1,0:T(8,128)(2,1)} %bitcast_select_fusion), calls=%async_computation | async-start | bytes 524288 | tf_op jit(solution)/shard_map/all_to_all | solution.py:128
Sparse Core Ops, SparseCore 0:
  36.1 9.8 all-gather.5
  57.3 11.7 all-gather.7
  87.4 41.3 all-gather.9
  130.7 38.8 all-gather.11
where the time goes:
time: 192 us
  waiting for transfers between devices  103 us (54%)
  blocking collectives  30 us (16%)
  matrix products  20.3 us (11%)
  other arithmetic  15.7 us (8%)
  between operations  13.4 us (7%)
  local copies, waits for them, and re-layouts  6.31 us (3%)
  starting transfers between devices  3.72 us (2%)
    all_gather x1, waiting for transfers between devices, local(): lax.all_gather(value_rows, 'seq', axis=0, tiled=True)  37.2 us
    all_gather x1, waiting for transfers between devices, local(): lax.all_gather(key_rows, 'seq', axis=0, tiled=True)  35.3 us
    all_gather x1, blocking collectives, local(): all_ids = lax.all_gather(byte_ids, 'seq', axis=0, tiled=True)  28.1 us
    all_gather x2, waiting for transfers between devices, local(): whole_rows = lax.all_gather(stream, 'head', axis=1, tiled=True)  21.8 us
    convert_element_type x2, other arithmetic, activate(): jax.nn.gelu(stream * rescale[:, None] * gain_row[None, :], approximate=Fa...  10.1 us
    all_to_all x1, waiting for transfers between devices, local(): lax.all_to_all(sectioned, 'seq', split_axis=0, concat_axis=0, tiled=True)  8.27 us
    reduce_sum x2, other arithmetic, local(): jnp.sum(whole_rows * whole_rows, axis=1)  3.9 us
    dot_general x2, matrix products, local(): jnp.dot(in_front, conv_weight[layer_index, 2], preferred_element_type=jnp...  3.87 us
  transfers between devices with their start and end apart: 5, of which 5 were waited for; matrix products, arithmetic and copies ran while one was open for 5% of the time, Pallas kernels for 0%

commit v1 on v0

--- a/solution.py
+++ b/solution.py
@@ -10,6 +10,22 @@
 DILATION_SECOND = 2048
 POOL = 8
 epsilon = 1e-05
+
+
+def collect(x, axis, dim):
+    ways, here, lap = (lax.axis_size(axis), lax.axis_index(axis), x.shape[dim])
+    dims = [n * ways if d == dim else n for d, n in enumerate(x.shape)]
+    full = lax.dynamic_update_slice_in_dim(jnp.zeros(dims, x.dtype), x, here * lap, axis=dim)
+    going_up = going_down = x
+    for far in range(1, ways // 2 + 1):
+        going_up = lax.ppermute(going_up, axis, [(d, (d + 1) % ways) for d in range(ways)])
+        full = lax.dynamic_update_slice_in_dim(full, going_up, (here - far) % ways * lap, axis=dim)
+        if 2 * far < ways:
+            going_down = lax.ppermute(going_down, axis, [(d, (d - 1) % ways) for d in range(ways)])
+            full = lax.dynamic_update_slice_in_dim(
+                full, going_down, (here + far) % ways * lap, axis=dim
+            )
+    return full
 
 
 def activate(stream, gain_row, squares):
@@ -100,10 +116,7 @@
     value_rows = jnp.dot(pooled_full, qkv_weight[2], preferred_element_type=jnp.float32).astype(
         jnp.bfloat16
     )
-    pieces = (
-        lax.all_gather(key_rows, "seq", axis=0, tiled=True),
-        lax.all_gather(value_rows, "seq", axis=0, tiled=True),
-    )
+    pieces = (collect(key_rows, "seq", 0), lax.all_gather(value_rows, "seq", axis=0, tiled=True))
     row_max, totals, weighted = attend(
         start_state,
         pieces[0],

time: 192 us -> 161 us (0.84)
  waiting for transfers between devices: 103 us -> 42.1 us
  starting transfers between devices: 3.72 us -> 20.5 us
  local copies, waits for them, and re-layouts: 6.31 us -> 18.8 us
    all_gather x1, waiting for transfers between devices: 37.2 us -> 0.02 us  [local(): lax.all_gather(value_rows, 'seq', axis=0, tiled=True)]
    all_gather x1 -> x0, waiting for transfers between devices: 35.3 us -> none  [local(): lax.all_gather(key_rows, 'seq', axis=0, tiled=True)]
    ppermute x0 -> x7, starting transfers between devices: none -> 14.4 us  [the longest x3 10.9 us: collect(): lax.ppermute(going_down, axis, [(d, (d - 1) % ways) for d in range(ways)])]
    dynamic_update_slice x0 -> x8, local copies, waits for them, and re-layouts: none -> 12.5 us  [the longest x4 6.07 us: collect(): lax.dynamic_update_slice_in_dim(full, going_up, (here - far) % ways * lap...]
    ppermute x0 -> x7, waiting for transfers between devices: none -> 12 us  [the longest x4 12 us: collect(): lax.ppermute(going_up, axis, [(d, (d + 1) % ways) for d in range(ways)])]
    all_to_all x1, starting transfers between devices: 3.41 us -> 6 us  [local(): lax.all_to_all(sectioned, 'seq', split_axis=0, concat_axis=0, tiled=True)]
  transfers between devices with their start and end apart: 5 -> 11, of which waited for: 5 -> 6; matrix products, arithmetic and copies ran while one was open for 5% -> 13% of each run, Pallas kernels for 0% -> 0%
where the time goes in v1:
time: 161 us; the launch traced here: 160 us
  waiting for transfers between devices  42.1 us (26%)
  blocking collectives  30 us (19%)
  starting transfers between devices  20.5 us (13%)
  matrix products  19.6 us (12%)
  local copies, waits for them, and re-layouts  18.8 us (12%)
  other arithmetic  15.6 us (10%)
  between operations  13.5 us (8%)
    all_gather x1, blocking collectives, local(): all_ids = lax.all_gather(byte_ids, 'seq', axis=0, tiled=True)  28.1 us
    all_gather x2, waiting for transfers between devices, local(): whole_rows = lax.all_gather(stream, 'head', axis=1, tiled=True)  21.8 us
    ppermute x4, waiting for transfers between devices, collect(): lax.ppermute(going_up, axis, [(d, (d + 1) % ways) for d in range(ways)])  12 us
    ppermute x3, starting transfers between devices, collect(): lax.ppermute(going_down, axis, [(d, (d - 1) % ways) for d in range(ways)])  10.9 us
    convert_element_type x2, other arithmetic, activate(): jax.nn.gelu(stream * rescale[:, None] * gain_row[None, :], approximate=Fa...  10.1 us
    all_to_all x1, waiting for transfers between devices, local(): lax.all_to_all(sectioned, 'seq', split_axis=0, concat_axis=0, tiled=True)  8.22 us
    dynamic_update_slice x4, local copies, waits for them, and re-layouts, collect(): lax.dynamic_update_slice_in_dim(full, going_up, (here - far) % ways * lap...  6.07 us
    all_to_all x1, starting transfers between devices, local(): lax.all_to_all(sectioned, 'seq', split_axis=0, concat_axis=0, tiled=True)  6 us
  transfers between devices with their start and end apart: 11, of which 6 were waited for; matrix products, arithmetic and copies ran while one was open for 13% of the time, Pallas kernels for 0%

profile of v1, /device:TPU:0, one launch (start us, length us, event | category | flops | bytes accessed | tf_op | source)
XLA Modules:
  0.0 160.0 jit_solution(13024990545040487658)
XLA Ops:
  6.6 28.1 %all-gather = s32[8,1,512]{2,1,0:T(1,128)S(1)} all-gather(s32[1,1,512]{2,1,0:T(1,128)} %bitcast.72), channel_id=1, replica_groups=mesh['groups'=2,'seq'=8,'head'=2] {'seq'}, dimensions={0}, use_global_device_ids=true | all-gather | bytes 18432 | tf_op jit(solution)/shard_map/all_gather | solution.py:71
  36.1 9.9 %all-gather.5.cloned.1.call-done = f32[512,1024]{1,0:T(8,128)} async-done(((f32[512,512]{1,0:T(8,128)}), f32[512,1024]{1,0:T(8,128)}) %all-gather.5.cloned.1.call-update) | async-done | bytes 2097168 | tf_op jit(solution)/shard_map/all_gather | solution.py:80
  46.0 2.0 %multiply_reduce_fusion.1 = f32[512]{0:T(512)S(1)} fusion(f32[512,1024]{1,0:T(8,128)} %all-gather.5.cloned.1.call-done), kind=kLoop, calls=%fused_computation.48 | loop fusion | flops 1048064 | bytes 2099200 | tf_op jit(solution)/shard_map/reduce_sum | solution.py:81
  48.2 5.1 %fusion.2 = bf16[512,1024]{1,0:T(8,128)(2,1)S(1)} fusion(f32[512,1024]{1,0:T(8,128)S(1)} %copy-done.2, f32[1024]{0:T(1024)S(1)} %bitcast.68, f32[512]{0:T(512)S(1)} %add_rsqrt_fusion.1), kind=kLoop, calls=%fused_computation.4 | loop fusion | flops 35127296 | bytes 3151872 | tf_op jit(solution)/shard_map/convert_element_type | solution.py:33
  57.2 11.9 %all-gather.7.cloned.1.call-done = f32[512,1024]{1,0:T(8,128)} async-done(((f32[512,512]{1,0:T(8,128)}), f32[512,1024]{1,0:T(8,128)}) %all-gather.7.cloned.1.call-update) | async-done | bytes 2097168 | tf_op jit(solution)/shard_map/all_gather | solution.py:80
  69.0 2.0 %multiply_reduce_fusion = f32[512]{0:T(512)S(1)} fusion(f32[512,1024]{1,0:T(8,128)} %all-gather.7.cloned.1.call-done), kind=kLoop, calls=%fused_computation.33 | loop fusion | flops 1048064 | bytes 2099200 | tf_op jit(solution)/shard_map/reduce_sum | solution.py:81
  71.3 5.1 %fusion.5 = bf16[512,1024]{1,0:T(8,128)(2,1)S(1)} fusion(f32[512,1024]{1,0:T(8,128)S(1)} %copy-done.3, f32[1024]{0:T(1024)S(1)} %bitcast.67, f32[512]{0:T(512)S(1)} %add_rsqrt_fusion), kind=kLoop, calls=%fused_computation.7 | loop fusion | flops 35127296 | bytes 3151872 | tf_op jit(solution)/shard_map/convert_element_type | solution.py:33
  76.4 1.9 %fusion.52 = f32[512,512]{1,0:T(8,128)S(1)} fusion(bf16[2,3,1024,512]{3,2,1,0:T(8,128)(2,1)} %param.9, bf16[256,1024]{1,0:T(8,128)(2,1)S(1)} %get-tuple-element.6), kind=kOutput, calls=%fused_computation.74 | convolution fusion | flops 536870912 | bytes 2621440 | tf_op jit(solution)/shard_map/dot_general | solution.py:84
  78.4 2.0 %convolution_add_fusion.1 = f32[512,512]{1,0:T(8,128)S(1)} fusion(f32[512,512]{1,0:T(8,128)S(1)} %fusion.52, bf16[512,1024]{1,0:T(8,128)(2,1)S(1)} %fusion.5, bf16[2,3,1024,512]{3,2,1,0:T(8,128)(2,1)} %param.9), kind=kOutput, calls=%fused_computation.58 | convolution fusion | flops 537133056 | bytes 4194304 | tf_op jit(solution)/shard_map/dot_general | solution.py:85
  80.4 2.2 %fusion.37 = f32[64,512]{1,0:T(8,128)S(1)} fusion(f32[512,512]{1,0:T(8,128)S(1)} %copy-done.4, f32[512,512]{1,0:T(8,128)S(1)} %convolution_add_fusion.1, bf16[2,3,1024,512]{3,2,1,0:T(8,128)(2,1)} %param.9, bf16[256,1024]{1,0:T(8,128)(2,1)S(1)} %get-tuple-element.5, f32[512]{0:T(512)S(1)} %bitcast.73), kind=kOutput, calls=%fused_computation.65 | convolution fusion | flops 537886720 | bytes 3803136 | tf_op jit(solution)/shard_map/dot_general | solution.py:88
  84.5 2.7 %fusion.45 = bf16[64,1024]{1,0:T(8,128)(2,1)} fusion(bf16[64,1024]{1,0:T(8,128)(2,1)S(1)} %all_gather.18, bf16[3,1024,1024]{2,1,0:T(8,128)(2,1)} %param.11), kind=kOutput, calls=%fused_computation.69 | convolution fusion | flops 134283264 | bytes 2359296 | tf_op jit(solution)/shard_map/dot_general | solution.py:116
  87.3 2.1 %fusion.42 = bf16[64,1024]{1,0:T(8,128)(2,1)S(1)} fusion(bf16[64,1024]{1,0:T(8,128)(2,1)S(1)} %all_gather.18, bf16[3,1024,1024]{2,1,0:T(8,128)(2,1)} %param.11), kind=kOutput, calls=%fused_computation.68 | convolution fusion | flops 134283264 | bytes 2359296 | tf_op jit(solution)/shard_map/dot_general | solution.py:113
  91.1 3.0 %collective-permute-start.1 = (bf16[64,1024]{1,0:T(8,128)(2,1)S(1)}, bf16[64,1024]{1,0:T(8,128)(2,1)S(1)}, u32[]{:S(2)}, u32[]{:S(2)}) collective-permute-start(bf16[64,1024]{1,0:T(8,128)(2,1)S(1)} %fusion.42), channel_id=1, source_target_pairs={{0,14},{2,0},{4,2},{6,4},{8,6},{10,8},{12,10},{14,12},{1,15},{3,1}... | collective-permute-start | bytes 393224 | tf_op jit(solution)/shard_map/ppermute | solution.py:24
  94.2 3.8 %collective-permute-done = bf16[64,1024]{1,0:T(8,128)(2,1)S(1)} collective-permute-done((bf16[64,1024]{1,0:T(8,128)(2,1)S(1)}, bf16[64,1024]{1,0:T(8,128)(2,1)S(1)}, u32[]{:S(2)}, u32[]{:S(2)}) %collective-permute-start) | collective-permute-done | bytes 131104 | tf_op jit(solution)/shard_map/ppermute | solution.py:21
  99.8 3.1 %collective-permute-start.3 = (bf16[64,1024]{1,0:T(8,128)(2,1)S(1)}, bf16[64,1024]{1,0:T(8,128)(2,1)S(1)}, u32[]{:S(2)}, u32[]{:S(2)}) collective-permute-start(bf16[64,1024]{1,0:T(8,128)(2,1)S(1)} %collective-permute-done.1), channel_id=1, source_target_pairs={{0,14},{2,0},{4,2},{6,4},{8,6},{10,8},{12,10},{14,12},{1,15},{3,1}... | collective-permute-start | bytes 393224 | tf_op jit(solution)/shard_map/ppermute | solution.py:24
  102.9 5.3 %collective-permute-done.2 = bf16[64,1024]{1,0:T(8,128)(2,1)S(1)} collective-permute-done((bf16[64,1024]{1,0:T(8,128)(2,1)S(1)}, bf16[64,1024]{1,0:T(8,128)(2,1)S(1)}, u32[]{:S(2)}, u32[]{:S(2)}) %collective-permute-start.2) | collective-permute-done | bytes 131104 | tf_op jit(solution)/shard_map/ppermute | solution.py:21
  108.3 4.8 %collective-permute-start.5 = (bf16[64,1024]{1,0:T(8,128)(2,1)S(1)}, bf16[64,1024]{1,0:T(8,128)(2,1)S(1)}, u32[]{:S(2)}, u32[]{:S(2)}) collective-permute-start(bf16[64,1024]{1,0:T(8,128)(2,1)S(1)} %collective-permute-done.3), channel_id=1, source_target_pairs={{0,14},{2,0},{4,2},{6,4},{8,6},{10,8},{12,10},{14,12},{1,15},{3,1}... | collective-permute-start | bytes 393224 | tf_op jit(solution)/shard_map/ppermute | solution.py:24
  113.1 2.9 %collective-permute-done.4 = bf16[64,1024]{1,0:T(8,128)(2,1)S(1)} collective-permute-done((bf16[64,1024]{1,0:T(8,128)(2,1)S(1)}, bf16[64,1024]{1,0:T(8,128)(2,1)S(1)}, u32[]{:S(2)}, u32[]{:S(2)}) %collective-permute-start.4) | collective-permute-done | bytes 131104 | tf_op jit(solution)/shard_map/ppermute | solution.py:21
  116.0 2.1 %fusion.39 = bf16[64,1024]{1,0:T(8,128)(2,1)S(1)} fusion(bf16[64,1024]{1,0:T(8,128)(2,1)S(1)} %all_gather.18, bf16[3,1024,1024]{2,1,0:T(8,128)(2,1)} %param.11), kind=kOutput, calls=%fused_computation.67 | convolution fusion | flops 134283264 | bytes 2359296 | tf_op jit(solution)/shard_map/dot_general | solution.py:95
  122.6 2.0 %dynamic_update_slice.26 = bf16[512,1024]{0,1:T(8,128)(2,1)S(1)} dynamic-update-slice(bf16[512,1024]{0,1:T(8,128)(2,1)S(1)} %dynamic_update_slice.25, bf16[64,1024]{0,1:T(8,128)(2,1)S(1)} %copy.30, s32[]{:T(128)S(6)} %select_n.164, s32[]{:T(128)} %constant.189.clone.1) | dynamic-update-slice | bytes 262148 | tf_op jit(solution)/shard_map/dynamic_update_slice | solution.py:25
  127.4 2.0 %dynamic_update_slice.29 = bf16[512,1024]{0,1:T(8,128)(2,1)S(1)} dynamic-update-slice(bf16[512,1024]{0,1:T(8,128)(2,1)S(1)} %dynamic_update_slice.28, bf16[64,1024]{0,1:T(8,128)(2,1)S(1)} %copy.33, s32[]{:T(128)S(6)} %select_n.170, s32[]{:T(128)} %constant.189.clone.1) | dynamic-update-slice | bytes 262148 | tf_op jit(solution)/shard_map/dynamic_update_slice | solution.py:22
  129.6 2.0 %dynamic_update_slice.30 = bf16[512,1024]{0,1:T(8,128)(2,1)S(1)} dynamic-update-slice(bf16[512,1024]{0,1:T(8,128)(2,1)S(1)} %dynamic_update_slice.29, bf16[64,1024]{0,1:T(8,128)(2,1)S(1)} %copy.34, s32[]{:T(128)S(6)} %select_n.172, s32[]{:T(128)} %constant.189.clone.1) | dynamic-update-slice | bytes 262148 | tf_op jit(solution)/shard_map/dynamic_update_slice | solution.py:25
  138.6 6.0 %all-to-all-start = ((bf16[8,16,1024]{2,1,0:T(8,128)(2,1)}), bf16[8,16,1024]{2,1,0:T(8,128)(2,1)S(1)}, u32[]{:S(2)}, u32[]{:S(2)}) async-start(bf16[8,16,1024]{2,1,0:T(8,128)(2,1)} %bitcast_select_fusion), calls=%async_computation | async-start | bytes 524288 | tf_op jit(solution)/shard_map/all_to_all | solution.py:141
  144.6 8.2 %all-to-all-done = bf16[8,16,1024]{2,1,0:T(8,128)(2,1)S(1)} async-done(((bf16[8,16,1024]{2,1,0:T(8,128)(2,1)}), bf16[8,16,1024]{2,1,0:T(8,128)(2,1)S(1)}, u32[]{:S(2)}, u32[]{:S(2)}) %all-to-all-start) | async-done | bytes 262176 | tf_op jit(solution)/shard_map/all_to_all | solution.py:141
  (74 shorter events, 26.5 us)
Async XLA Ops:
  6.5 28.1 %copy-start = (bf16[256,512]{1,0:T(8,128)(2,1)S(1)}, bf16[256,512]{1,0:T(8,128)(2,1)}, u32[]{:S(2)}) copy-start(bf16[256,512]{1,0:T(8,128)(2,1)} %param.7) | copy-start | bytes 786436
  6.5 29.5 %copy-start.7 = (f32[2,512]{1,0:T(2,128)S(1)}, f32[2,512]{1,0:T(2,128)}, u32[]{:S(2)}) copy-start(f32[2,512]{1,0:T(2,128)} %param.10) | copy-start | bytes 12292
  6.5 29.5 %copy-start.6 = (f32[2,1024]{1,0:T(2,128)S(1)}, f32[2,1024]{1,0:T(2,128)}, u32[]{:S(2)}) copy-start(f32[2,1024]{1,0:T(2,128)} %param.8) | copy-start | bytes 24580
  6.5 39.5 %all-gather.5.cloned.1.call-start = ((), (), s32[]{:S(2)}) async-start(), calls=%async_computation.1 | async-start | bytes 3145728 | tf_op jit(solution)/shard_map/all_gather | solution.py:80
  36.0 33.1 %all-gather.7.cloned.1.call-start = ((), (), s32[]{:S(2)}) async-start(), calls=%async_computation.2 | async-start | bytes 3145728 | tf_op jit(solution)/shard_map/all_gather | solution.py:80
  46.0 2.2 %copy-start.2 = (f32[512,1024]{1,0:T(8,128)S(1)}, f32[512,1024]{1,0:T(8,128)}, u32[]{:S(2)}) copy-start(f32[512,1024]{1,0:T(8,128)} %all-gather.5.cloned.1.call-done) | copy-start | bytes 6291460
  48.2 5.3 %copy-start.5 = (bf16[2,3,1024,512]{3,2,1,0:T(8,128)(2,1)S(1)}, bf16[2,3,1024,512]{3,2,1,0:T(8,128)(2,1)}, u32[]{:S(2)}) copy-start(bf16[2,3,1024,512]{3,2,1,0:T(8,128)(2,1)} %param.9) | copy-start | bytes 18874372
  54.2 1.2 copy-start.1
  57.1 78.1 %all-gather.9.cloned.1.call-start = ((), (), s32[]{:S(2)}) async-start(), calls=%async_computation.3 | async-start | bytes 1179648 | tf_op jit(solution)/shard_map/all_gather | solution.py:119
  69.0 2.2 %copy-start.3 = (f32[512,1024]{1,0:T(8,128)S(1)}, f32[512,1024]{1,0:T(8,128)}, u32[]{:S(2)}) copy-start(f32[512,1024]{1,0:T(8,128)} %all-gather.7.cloned.1.call-done) | copy-start | bytes 6291460
  78.3 2.0 %copy-start.4 = (f32[512,512]{1,0:T(8,128)S(1)}, f32[512,512]{1,0:T(8,128)}, u32[]{:S(2)}) copy-start(f32[512,512]{1,0:T(8,128)} %fusion.34) | copy-start | bytes 3145732
  89.3 8.6 %collective-permute-start = (bf16[64,1024]{1,0:T(8,128)(2,1)S(1)}, bf16[64,1024]{1,0:T(8,128)(2,1)S(1)}, u32[]{:S(2)}, u32[]{:S(2)}) collective-permute-start(bf16[64,1024]{1,0:T(8,128)(2,1)S(1)} %fusion.42), channel_id=1, source_target_pairs={{0,2},{2,4},{4,6},{6,8},{8,10},{10,12},{12,14},{14,0},{1,3},{3,5},... | collective-permute-start | bytes 393224 | tf_op jit(solution)/shard_map/ppermute | solution.py:21
  91.1 8.7 %collective-permute-start.1 = (bf16[64,1024]{1,0:T(8,128)(2,1)S(1)}, bf16[64,1024]{1,0:T(8,128)(2,1)S(1)}, u32[]{:S(2)}, u32[]{:S(2)}) collective-permute-start(bf16[64,1024]{1,0:T(8,128)(2,1)S(1)} %fusion.42), channel_id=1, source_target_pairs={{0,14},{2,0},{4,2},{6,4},{8,6},{10,8},{12,10},{14,12},{1,15},{3,1}... | collective-permute-start | bytes 393224 | tf_op jit(solution)/shard_map/ppermute | solution.py:24
  98.0 10.2 %collective-permute-start.2 = (bf16[64,1024]{1,0:T(8,128)(2,1)S(1)}, bf16[64,1024]{1,0:T(8,128)(2,1)S(1)}, u32[]{:S(2)}, u32[]{:S(2)}) collective-permute-start(bf16[64,1024]{1,0:T(8,128)(2,1)S(1)} %collective-permute-done), channel_id=1, source_target_pairs={{0,2},{2,4},{4,6},{6,8},{8,10},{10,12},{12,14},{14,0},{1,3},{3,5},... | collective-permute-start | bytes 393224 | tf_op jit(solution)/shard_map/ppermute | solution.py:21
  99.8 8.5 %collective-permute-start.3 = (bf16[64,1024]{1,0:T(8,128)(2,1)S(1)}, bf16[64,1024]{1,0:T(8,128)(2,1)S(1)}, u32[]{:S(2)}, u32[]{:S(2)}) collective-permute-start(bf16[64,1024]{1,0:T(8,128)(2,1)S(1)} %collective-permute-done.1), channel_id=1, source_target_pairs={{0,14},{2,0},{4,2},{6,4},{8,6},{10,8},{12,10},{14,12},{1,15},{3,1}... | collective-permute-start | bytes 393224 | tf_op jit(solution)/shard_map/ppermute | solution.py:24
  108.2 7.8 %collective-permute-start.4 = (bf16[64,1024]{1,0:T(8,128)(2,1)S(1)}, bf16[64,1024]{1,0:T(8,128)(2,1)S(1)}, u32[]{:S(2)}, u32[]{:S(2)}) collective-permute-start(bf16[64,1024]{1,0:T(8,128)(2,1)S(1)} %collective-permute-done.2), channel_id=1, source_target_pairs={{0,2},{2,4},{4,6},{6,8},{8,10},{10,12},{12,14},{14,0},{1,3},{3,5},... | collective-permute-start | bytes 393224 | tf_op jit(solution)/shard_map/ppermute | solution.py:21
  108.3 21.1 %collective-permute-start.5 = (bf16[64,1024]{1,0:T(8,128)(2,1)S(1)}, bf16[64,1024]{1,0:T(8,128)(2,1)S(1)}, u32[]{:S(2)}, u32[]{:S(2)}) collective-permute-start(bf16[64,1024]{1,0:T(8,128)(2,1)S(1)} %collective-permute-done.3), channel_id=1, source_target_pairs={{0,14},{2,0},{4,2},{6,4},{8,6},{10,8},{12,10},{14,12},{1,15},{3,1}... | collective-permute-start | bytes 393224 | tf_op jit(solution)/shard_map/ppermute | solution.py:24
  116.0 15.7 %collective-permute-start.6 = (bf16[64,1024]{1,0:T(8,128)(2,1)S(1)}, bf16[64,1024]{1,0:T(8,128)(2,1)S(1)}, u32[]{:S(2)}, u32[]{:S(2)}) collective-permute-start(bf16[64,1024]{1,0:T(8,128)(2,1)S(1)} %collective-permute-done.4), channel_id=1, source_target_pairs={{0,2},{2,4},{4,6},{6,8},{8,10},{10,12},{12,14},{14,0},{1,3},{3,5},... | collective-permute-start | bytes 393224 | tf_op jit(solution)/shard_map/ppermute | solution.py:21
  138.6 14.2 %all-to-all-start = ((bf16[8,16,1024]{2,1,0:T(8,128)(2,1)}), bf16[8,16,1024]{2,1,0:T(8,128)(2,1)S(1)}, u32[]{:S(2)}, u32[]{:S(2)}) async-start(bf16[8,16,1024]{2,1,0:T(8,128)(2,1)} %bitcast_select_fusion), calls=%async_computation | async-start | bytes 524288 | tf_op jit(solution)/shard_map/all_to_all | solution.py:141
Sparse Core Ops, SparseCore 0:
  36.1 9.8 all-gather.4
  57.3 11.7 all-gather.6
  87.4 44.0 all-gather.8
